TPU v7x, 256 devices: a whole 4x4x8 slice. The times are simulated.
256 devices in a mesh: seq: 32 (over z_lo, y, core), chan: 8 (over x, z_hi).
Axes of the slice: x: 4, y: 4, z: 8 (z_hi: 2, z_lo: 4; z = z_hi * 4 + z_lo), core: 2. Of those that a mesh axis runs over, the one named last changes fastest.
Arguments:
- query_proj: bfloat16 [128, 131072], P('chan', 'seq'), may hold values from -6 to 6
- key_proj: bfloat16 [128, 131072], P('chan', 'seq'), may hold values from -6 to 6
- value_proj: bfloat16 [128, 131072], P('chan', 'seq'), may hold values from -6 to 6
- filter_taps: float32 [128, 131072], P('chan', 'seq'), may hold values from -1.1 to 1.1
- skip_bias: float32 [128], P('chan'), may hold values from -2.5 to 2.5
Outputs:
- hyena_out: float32 [128, 131072], P(None, ('seq', 'chan'))
All inputs are finite; a program needn't handle non-finite values.
Results may differ from a plain program's by a relative error of at most 0.0003.
Values sent between devices are 32-bit elements; how exact they have to be, the bound alone decides.
A program may use at most 64 MiB of HBM per device.

v0:
```python
import math

import jax
import jax.numpy as jnp
from jax import lax
from jax.sharding import PartitionSpec as P

HIGHEST = lax.Precision.HIGHEST


def swapped(block, axis, distance):
    count = lax.axis_size(axis)
    route = []
    for low in range(count):
        high = low | 1 << distance
        if high != low and high < count:
            route += [(low, high), (high, low)]
    return lax.ppermute(block, axis, route)


def phase_table(exponent, modulus, direction):
    angles = direction * 2.0 * math.pi / modulus * (exponent % modulus).astype(jnp.float32)
    return (jnp.cos(angles), jnp.sin(angles))


def transform_table(length, direction):
    counter = jnp.arange(length, dtype=jnp.int32)
    return phase_table(counter[:, None] * counter[None, :], length, direction)


def rotate(current, cos_part, sin_part):
    real_part = current[0] * cos_part - current[1] * sin_part
    imag_part = current[0] * sin_part + current[1] * cos_part
    return jnp.stack([real_part, imag_part])


def apply_table(current, tables, formula, table_first):
    cos_part, sin_part = tables

    def contract(matrix, operand):
        if table_first:
            return jnp.einsum(formula, matrix, operand, precision=HIGHEST)
        return jnp.einsum(formula, operand, matrix, precision=HIGHEST)

    real_part = contract(cos_part, current[0]) - contract(sin_part, current[1])
    imag_part = contract(cos_part, current[1]) + contract(sin_part, current[0])
    return jnp.stack([real_part, imag_part])


def paired(raw, cos_part, sin_part, axis_pos):
    imag_in = jnp.zeros_like(raw)
    real_part = jnp.stack([raw, raw * cos_part - imag_in * sin_part], axis=axis_pos)
    imag_part = jnp.stack([imag_in, raw * sin_part + imag_in * cos_part], axis=axis_pos)
    return jnp.stack([real_part, imag_part])


def split_sizes(tokens_here):
    digits = tokens_here.bit_length() - 1
    outer = 2 ** ((digits + 1) // 2)
    return (outer, tokens_here // outer)


def forward_local(current):
    tokens_here = current.shape[-1]
    outer, columns = split_sizes(tokens_here)
    blocks = current.reshape(current.shape[:-1] + (outer, columns))
    blocks = apply_table(blocks, transform_table(outer, -1), "ka,...ab->...kb", True)
    row_index = jnp.arange(outer, dtype=jnp.int32)[:, None]
    col_index = jnp.arange(columns, dtype=jnp.int32)[None, :]
    cos_part, sin_part = phase_table(row_index * col_index, tokens_here, -1)
    blocks = rotate(blocks, cos_part, sin_part)
    return apply_table(blocks, transform_table(columns, -1), "...kb,lb->...kl", False)


def inverse_local(spectrum):
    outer = spectrum.shape[-2]
    columns = spectrum.shape[-1]
    tokens_here = outer * columns
    blocks = apply_table(spectrum, transform_table(columns, 1), "...kl,bl->...kb", False)
    row_index = jnp.arange(outer, dtype=jnp.int32)[:, None]
    col_index = jnp.arange(columns, dtype=jnp.int32)[None, :]
    cos_part, sin_part = phase_table(row_index * col_index, tokens_here, 1)
    blocks = rotate(blocks, cos_part, sin_part)
    blocks = apply_table(blocks, transform_table(outer, 1), "ak,...kb->...ab", True)
    return blocks.reshape(blocks.shape[:-2] + (tokens_here,))


def reversed_bits(my_index, levels):
    reversed_index = jnp.zeros((), jnp.int32)
    for bit_number in range(levels):
        reversed_index = reversed_index + ((my_index >> bit_number & 1) << levels - 1 - bit_number)
    return reversed_index


def final_part(first_half, second_half, cos_part, sin_part):
    return first_half[0] + cos_part * second_half[0] - sin_part * second_half[1]


def butterfly_forward(sources, my_index, levels):
    devices = 2**levels
    half_span = devices // 2
    top_bit = levels - 1
    partner = swapped(sources, "seq", top_bit)
    is_lower = my_index >> top_bit & 1 == 0
    lower_raw = jnp.where(is_lower, sources, partner)
    upper_raw = jnp.where(is_lower, partner, sources)
    lower_index = my_index & half_span - 1
    lower_cos, lower_sin = phase_table(lower_index, 2 * devices, -1)
    upper_cos, upper_sin = phase_table(lower_index + half_span, 2 * devices, -1)
    lower_pair = paired(lower_raw, lower_cos, lower_sin, 0)
    upper_pair = paired(upper_raw, upper_cos, upper_sin, 0)
    sign_part = jnp.where(is_lower, 1.0, -1.0).astype(jnp.float32)
    cos_part, sin_part = phase_table(lower_index, devices, -1)
    current = rotate(
        lower_pair + sign_part * upper_pair,
        jnp.where(is_lower, 1.0, cos_part),
        jnp.where(is_lower, 0.0, sin_part),
    )
    for bit_number in range(top_bit - 1, -1, -1):
        other = swapped(current, "seq", bit_number)
        stride = 2**bit_number
        is_lower = my_index >> bit_number & 1 == 0
        sign_part = jnp.where(is_lower, 1.0, -1.0).astype(jnp.float32)
        cos_part, sin_part = phase_table(my_index & stride - 1, 2 * stride, -1)
        current = rotate(
            sign_part * current + other,
            jnp.where(is_lower, 1.0, cos_part),
            jnp.where(is_lower, 0.0, sin_part),
        )
    return current


def butterfly_inverse(current, my_index, levels):
    for bit_number in range(levels):
        other = swapped(current, "seq", bit_number)
        stride = 2**bit_number
        is_lower = my_index >> bit_number & 1 == 0
        cos_part, sin_part = phase_table(my_index & stride - 1, 2 * stride, 1)
        kept_term = jnp.where(is_lower, current, other)
        scaled = rotate(jnp.where(is_lower, other, current), cos_part, sin_part)
        current = kept_term + jnp.where(is_lower, 1.0, -1.0).astype(jnp.float32) * scaled
    cos_part, sin_part = phase_table(my_index, 2 * 2**levels, 1)
    return final_part(current[:, 0], current[:, 1], cos_part, sin_part)


def body(query_proj, key_proj, value_proj, filter_taps, skip_bias):
    tokens_here = key_proj.shape[1]
    devices = lax.axis_size("seq")
    levels = devices.bit_length() - 1
    my_index = lax.axis_index("seq")
    length = 2 * devices * tokens_here
    gated_input = key_proj.astype(jnp.float32) * value_proj.astype(jnp.float32)
    tap_scale = 1.0
    sources = jnp.stack([gated_input, filter_taps * tap_scale])
    current = butterfly_forward(sources, my_index, levels)
    owner = reversed_bits(my_index, levels)
    parity = jnp.arange(2, dtype=jnp.int32)
    positions = jnp.arange(tokens_here, dtype=jnp.int32)
    exponent = (2 * owner + parity)[:, None] * positions[None, :]
    cos_part, sin_part = phase_table(exponent, length, -1)
    current = rotate(current, cos_part[:, None, None, :], sin_part[:, None, None, :])
    spectra = forward_local(current)
    signal = spectra[:, :, 0]
    filter_spec = spectra[:, :, 1]
    product = jnp.stack(
        [
            signal[0] * filter_spec[0] - signal[1] * filter_spec[1],
            signal[0] * filter_spec[1] + signal[1] * filter_spec[0],
        ]
    )
    back = inverse_local(product)
    cos_part, sin_part = phase_table(exponent, length, 1)
    back = rotate(back, cos_part[:, None, :], sin_part[:, None, :])
    convolved = butterfly_inverse(back, my_index, levels)
    convolved = convolved / length
    result = query_proj.astype(jnp.float32) * (convolved + skip_bias[:, None] * gated_input)
    return lax.all_to_all(result, "chan", split_axis=1, concat_axis=0, tiled=True)


def solution(mesh):
    placed = (P("chan", "seq"), P("chan", "seq"), P("chan", "seq"), P("chan", "seq"), P("chan"))
    return jax.shard_map(
        body, mesh=mesh, in_specs=placed, out_specs=P(None, ("seq", "chan")), check_vma=False
    )
```

profile of v0, /device:TPU:8, one launch (start us, length us, event | category | flops | bytes accessed | tf_op | source)
XLA Modules:
  0.0 400.7 jit_solution(16376987851758946043)
XLA Ops:
  2.0 3.4 collective-permute-start
  5.8 22.7 %collective-permute-done = f32[2,16,4096]{2,1,0:T(8,128)S(1)} collective-permute-done((f32[2,16,4096]{2,1,0:T(8,128)S(1)}, f32[2,16,4096]{2,1,0:T(8,128)S(1)}, u32[]{:S(2)}, u32[]{:S(2)}) %collective-permute-start) | collective-permute-done | bytes 524320 | tf_op jit(solution)/shard_map/ppermute | solution.py:18
  33.1 46.2 %collective-permute-done.1 = f32[2,2,2,16,4096]{4,3,2,1,0:T(8,128)} collective-permute-done((f32[2,2,2,16,4096]{4,3,2,1,0:T(8,128)}, f32[2,2,2,16,4096]{4,3,2,1,0:T(8,128)}, u32[]{:S(2)}, u32[]{:S(2)}) %collective-permute-start.1) | collective-permute-done | bytes 2097184 | tf_op jit(solution)/shard_map/ppermute | solution.py:18
  85.4 45.2 %collective-permute-done.2 = f32[2,2,2,16,4096]{4,3,2,1,0:T(8,128)} collective-permute-done((f32[2,2,2,16,4096]{4,3,2,1,0:T(8,128)}, f32[2,2,2,16,4096]{4,3,2,1,0:T(8,128)}, u32[]{:S(2)}, u32[]{:S(2)}) %collective-permute-start.2) | collective-permute-done | bytes 2097184 | tf_op jit(solution)/shard_map/ppermute | solution.py:18
  134.9 44.7 %collective-permute-done.3 = f32[2,2,2,16,4096]{4,3,2,1,0:T(8,128)} collective-permute-done((f32[2,2,2,16,4096]{4,3,2,1,0:T(8,128)}, f32[2,2,2,16,4096]{4,3,2,1,0:T(8,128)}, u32[]{:S(2)}, u32[]{:S(2)}) %collective-permute-start.3) | collective-permute-done | bytes 2097184 | tf_op jit(solution)/shard_map/ppermute | solution.py:18
  184.9 2.8 collective-permute-done.4
  196.1 3.0 copy.41
  199.1 4.0 %fusion.30 = f32[2,2,16,64,64]{4,3,2,1,0:T(8,128)S(1)} fusion(f32[2,64,64]{1,2,0:T(8,128)S(1)} %get-tuple-element.36, f32[2,64,64]{1,2,0:T(8,128)S(1)} %get-tuple-element.35, f32[2,2,16,64,64]{3,4,2,1,0:T(8,128)} %copy.41, f32[2,2,16,64,64]{3,4,2,1,0:T(8,128)S(1)} %copy.40, f32[]{:T(128)S(6)} %select_n.284), kind=kOutput, calls=%fused_computation.105 | convolution fusion | flops 203218944 | bytes 3211268 | tf_op jit(solution)/shard_map/ka,...ab->...kb/dot_general | solution.py:42
  210.3 3.9 fusion.19
  214.1 3.6 fusion.15
  217.8 3.7 subtract_bitcast_fusion
  221.5 3.7 add_bitcast_fusion
  234.2 2.9 fusion.3
  237.1 2.5 copy.53
  242.0 3.0 fusion.2
  247.4 2.5 collective-permute-done.5
  252.2 24.7 %collective-permute-done.6 = f32[2,2,16,4096]{3,2,1,0:T(8,128)} collective-permute-done((f32[2,2,16,4096]{3,2,1,0:T(8,128)}, f32[2,2,16,4096]{3,2,1,0:T(8,128)}, u32[]{:S(2)}, u32[]{:S(2)}) %collective-permute-start.6) | collective-permute-done | bytes 1048608 | tf_op jit(solution)/shard_map/ppermute | solution.py:18
  279.9 2.4 collective-permute-start.7
  282.5 23.4 %collective-permute-done.7 = f32[2,2,16,4096]{3,2,1,0:T(8,128)S(1)} collective-permute-done((f32[2,2,16,4096]{3,2,1,0:T(8,128)S(1)}, f32[2,2,16,4096]{3,2,1,0:T(8,128)S(1)}, u32[]{:S(2)}, u32[]{:S(2)}) %collective-permute-start.7) | collective-permute-done | bytes 1048608 | tf_op jit(solution)/shard_map/ppermute | solution.py:18
  306.3 3.2 collective-permute-start.8
  309.7 21.6 %collective-permute-done.8 = f32[2,2,16,4096]{3,2,1,0:T(8,128)S(1)} collective-permute-done((f32[2,2,16,4096]{3,2,1,0:T(8,128)S(1)}, f32[2,2,16,4096]{3,2,1,0:T(8,128)S(1)}, u32[]{:S(2)}, u32[]{:S(2)}) %collective-permute-start.8) | collective-permute-done | bytes 1048608 | tf_op jit(solution)/shard_map/ppermute | solution.py:18
  331.7 4.1 %collective-permute-start.9 = (f32[2,2,16,4096]{3,2,1,0:T(8,128)S(1)}, f32[2,2,16,4096]{3,2,1,0:T(8,128)S(1)}, u32[]{:S(2)}, u32[]{:S(2)}) collective-permute-start(f32[2,2,16,4096]{3,2,1,0:T(8,128)S(1)} %fusion.7), channel_id=1, source_target_pairs={{0,128},{128,0},{8,136},{136,8},{16,144},{144,16},{24,152},{152,24... | collective-permute-start | bytes 3145736 | tf_op jit(solution)/shard_map/ppermute | solution.py:18
  336.1 42.9 %collective-permute-done.9 = f32[2,2,16,4096]{3,2,1,0:T(8,128)S(1)} collective-permute-done((f32[2,2,16,4096]{3,2,1,0:T(8,128)S(1)}, f32[2,2,16,4096]{3,2,1,0:T(8,128)S(1)}, u32[]{:S(2)}, u32[]{:S(2)}) %collective-permute-start.9) | collective-permute-done | bytes 1048608 | tf_op jit(solution)/shard_map/ppermute | solution.py:18
  380.4 19.4 %all_to_all.19 = f32[16,8,512]{2,0,1:T(8,128)S(1)} all-to-all(f32[16,8,512]{2,0,1:T(8,128)S(1)} %bitcast.130), channel_id=1, replica_groups=mesh['seq'=32,'chan'=8] {'chan'}, dimensions={1} | all-to-all | bytes 524288 | tf_op jit(solution)/shard_map/all_to_all | solution.py:177
  (93 shorter events, 58.6 us)
Async XLA Ops:
  2.0 26.5 %collective-permute-start = (f32[2,16,4096]{2,1,0:T(8,128)S(1)}, f32[2,16,4096]{2,1,0:T(8,128)S(1)}, u32[]{:S(2)}, u32[]{:S(2)}) collective-permute-start(f32[2,16,4096]{2,1,0:T(8,128)S(1)} %pad_maximum_fusion.5), channel_id=1, source_target_pairs={{0,128},{128,0},{8,136},{136,8},{16,144},{144,16},{24,152},{152,24... | collective-permute-start | bytes 1572872 | tf_op jit(solution)/shard_map/ppermute | solution.py:18
  32.2 47.1 %collective-permute-start.1 = (f32[2,2,2,16,4096]{4,3,2,1,0:T(8,128)}, f32[2,2,2,16,4096]{4,3,2,1,0:T(8,128)}, u32[]{:S(2)}, u32[]{:S(2)}) collective-permute-start(f32[2,2,2,16,4096]{4,3,2,1,0:T(8,128)} %pad_maximum_fusion), channel_id=1, source_target_pairs={{0,64},{64,0},{8,72},{72,8},{16,80},{80,16},{24,88},{88,24},{32,96... | collective-permute-start | bytes 6291464 | tf_op jit(solution)/shard_map/ppermute | solution.py:18
  83.0 47.7 %collective-permute-start.2 = (f32[2,2,2,16,4096]{4,3,2,1,0:T(8,128)}, f32[2,2,2,16,4096]{4,3,2,1,0:T(8,128)}, u32[]{:S(2)}, u32[]{:S(2)}) collective-permute-start(f32[2,2,2,16,4096]{4,3,2,1,0:T(8,128)} %pad_maximum_fusion.1), channel_id=1, source_target_pairs={{0,32},{32,0},{8,40},{40,8},{16,48},{48,16},{24,56},{56,24},{64,96... | collective-permute-start | bytes 6291464 | tf_op jit(solution)/shard_map/ppermute | solution.py:18
  134.3 45.3 %collective-permute-start.3 = (f32[2,2,2,16,4096]{4,3,2,1,0:T(8,128)}, f32[2,2,2,16,4096]{4,3,2,1,0:T(8,128)}, u32[]{:S(2)}, u32[]{:S(2)}) collective-permute-start(f32[2,2,2,16,4096]{4,3,2,1,0:T(8,128)} %pad_maximum_fusion.2), channel_id=1, source_target_pairs={{0,16},{16,0},{8,24},{24,8},{32,48},{48,32},{40,56},{56,40},{64,80... | collective-permute-start | bytes 6291464 | tf_op jit(solution)/shard_map/ppermute | solution.py:18
  183.3 4.5 %collective-permute-start.4 = (f32[2,2,2,16,4096]{4,3,2,1,0:T(8,128)}, f32[2,2,2,16,4096]{4,3,2,1,0:T(8,128)}, u32[]{:S(2)}, u32[]{:S(2)}) collective-permute-start(f32[2,2,2,16,4096]{4,3,2,1,0:T(8,128)} %pad_maximum_fusion.3), channel_id=1, source_target_pairs={{0,8},{8,0},{16,24},{24,16},{32,40},{40,32},{48,56},{56,48},{64,72... | collective-permute-start | bytes 6291464 | tf_op jit(solution)/shard_map/ppermute | solution.py:18
  199.1 4.1 %copy-start = (f32[2,2,16,64,64]{3,4,2,1,0:T(8,128)S(1)}, f32[2,2,16,64,64]{3,4,2,1,0:T(8,128)}, u32[]{:S(2)}) copy-start(f32[2,2,16,64,64]{3,4,2,1,0:T(8,128)} %copy.41) | copy-start | bytes 3145732
  245.0 2.0 copy-start.5
  247.2 2.7 collective-permute-start.5
  250.1 26.8 %copy-start.1 = (f32[1,2,16,4096]{3,2,1,0:T(8,128)}, f32[1,2,16,4096]{3,2,1,0:T(8,128)S(1)}, u32[]{:S(2)}) copy-start(f32[1,2,16,4096]{3,2,1,0:T(8,128)S(1)} %get-tuple-element.31) | copy-start | bytes 1572868
  250.1 26.8 %copy-start.3 = (f32[1,2,16,4096]{3,2,1,0:T(8,128)}, f32[1,2,16,4096]{3,2,1,0:T(8,128)S(1)}, u32[]{:S(2)}) copy-start(f32[1,2,16,4096]{3,2,1,0:T(8,128)S(1)} %get-tuple-element.32) | copy-start | bytes 1572868
  251.4 25.5 %collective-permute-start.6 = (f32[2,2,16,4096]{3,2,1,0:T(8,128)}, f32[2,2,16,4096]{3,2,1,0:T(8,128)}, u32[]{:S(2)}, u32[]{:S(2)}) collective-permute-start(f32[2,2,16,4096]{3,2,1,0:T(8,128)} %fusion.4), channel_id=1, source_target_pairs={{0,16},{16,0},{8,24},{24,8},{32,48},{48,32},{40,56},{56,40},{64,80... | collective-permute-start | bytes 3145736 | tf_op jit(solution)/shard_map/ppermute | solution.py:18
  277.1 1.0 copy-start.2
  277.1 1.2 copy-start.4
  279.9 26.0 %collective-permute-start.7 = (f32[2,2,16,4096]{3,2,1,0:T(8,128)S(1)}, f32[2,2,16,4096]{3,2,1,0:T(8,128)S(1)}, u32[]{:S(2)}, u32[]{:S(2)}) collective-permute-start(f32[2,2,16,4096]{3,2,1,0:T(8,128)S(1)} %fusion.5), channel_id=1, source_target_pairs={{0,32},{32,0},{8,40},{40,8},{16,48},{48,16},{24,56},{56,24},{64,96... | collective-permute-start | bytes 3145736 | tf_op jit(solution)/shard_map/ppermute | solution.py:18
  306.3 24.9 %collective-permute-start.8 = (f32[2,2,16,4096]{3,2,1,0:T(8,128)S(1)}, f32[2,2,16,4096]{3,2,1,0:T(8,128)S(1)}, u32[]{:S(2)}, u32[]{:S(2)}) collective-permute-start(f32[2,2,16,4096]{3,2,1,0:T(8,128)S(1)} %fusion.6), channel_id=1, source_target_pairs={{0,64},{64,0},{8,72},{72,8},{16,80},{80,16},{24,88},{88,24},{32,96... | collective-permute-start | bytes 3145736 | tf_op jit(solution)/shard_map/ppermute | solution.py:18
  331.7 47.4 %collective-permute-start.9 = (f32[2,2,16,4096]{3,2,1,0:T(8,128)S(1)}, f32[2,2,16,4096]{3,2,1,0:T(8,128)S(1)}, u32[]{:S(2)}, u32[]{:S(2)}) collective-permute-start(f32[2,2,16,4096]{3,2,1,0:T(8,128)S(1)} %fusion.7), channel_id=1, source_target_pairs={{0,128},{128,0},{8,136},{136,8},{16,144},{144,16},{24,152},{152,24... | collective-permute-start | bytes 3145736 | tf_op jit(solution)/shard_map/ppermute | solution.py:18
  379.2 0.9 copy-start.6
  379.3 1.0 copy-start.7
  379.3 1.0 copy-start.8
  379.3 1.0 copy-start.9
where the time goes:
time: 409 us; the launch traced here: 401 us
  waiting for transfers between devices  277 us (68%)
  matrix products  40 us (10%)
  other arithmetic  25.4 us (6%)
  blocking collectives  19.4 us (5%)
  local copies, waits for them, and re-layouts  19.3 us (5%)
  starting transfers between devices  17.3 us (4%)
    ppermute x10, waiting for transfers between devices, swapped(): return lax.ppermute(block, axis, route)  277 us
    dot_general x8, matrix products, contract(): return jnp.einsum(formula, matrix, operand, precision=HIGHEST)  20.8 us
    all_to_all x1, blocking collectives, body(): lax.all_to_all(result, 'chan', split_axis=1, concat_axis=0, tiled=True)  19.4 us
    dot_general x8, matrix products, contract(): return jnp.einsum(formula, operand, matrix, precision=HIGHEST)  19.2 us
    ppermute x10, starting transfers between devices, swapped(): return lax.ppermute(block, axis, route)  17.3 us
    squeeze x6, local copies, waits for them, and re-layouts, rotate(): real_part = current[0] * cos_part - current[1] * sin_part  12.1 us
  transfers between devices with their start and end apart: 10, of which 10 were waited for; matrix products, arithmetic and copies ran while one was open for 0% of the time, Pallas kernels for 0%

commit v1 on v0

v1 whole, which is shorter than its diff:
```python
import math

import jax
import jax.numpy as jnp
import ml_dtypes
import numpy as np
from jax import lax
from jax.experimental import pallas as pl
from jax.experimental.pallas import tpu as pltpu
from jax.sharding import PartitionSpec as P

MESH = pl.DeviceIdType.MESH
F32 = jnp.float32
BF16 = jnp.bfloat16

ROWS = 512
COLS = 256
LENGTH = ROWS * COLS
CHIPS = 16
GROUPS = 8
HALF = ROWS // 2


def halves(table):
    high = table.astype(np.float32).astype(ml_dtypes.bfloat16)
    low = (table - high.astype(np.float64)).astype(np.float32).astype(ml_dtypes.bfloat16)
    return np.stack([high, low], axis=-3)


def tables():
    n1 = np.arange(ROWS, dtype=np.int64)
    n2 = np.arange(COLS, dtype=np.int64)
    angle = 2.0 * math.pi * (n2[:, None] * n2[None, :] % COLS) / COLS
    cos, sin = np.cos(angle), np.sin(angle)
    second = halves(np.block([[cos, -sin], [sin, cos]]))
    second_back = halves(np.block([[cos, sin], [-sin, cos]]))
    first, first_back, twiddle = [], [], []
    for core in range(2):
        k1 = core * HALF + np.arange(HALF, dtype=np.int64)
        angle = 2.0 * math.pi * (n1[None, :] * (4 * k1[:, None] + 1) % (4 * ROWS)) / (4 * ROWS)
        first.append(np.concatenate([np.cos(angle), -np.sin(angle)], axis=0))
        order = []
        for owner in (core, 1 - core):
            for bit in range(2):
                for chip in range(CHIPS):
                    for group in range(GROUPS):
                        order.append(((2 * chip + owner) * GROUPS + group) * 2 + bit)
        back = np.concatenate([np.cos(angle), -np.sin(angle)], axis=0).T / LENGTH
        first_back.append(back[np.array(order)])
        angle = 2.0 * math.pi * (n2[None, :] * (4 * k1[:, None] + 1) % (4 * LENGTH)) / (4 * LENGTH)
        twiddle.append(np.stack([np.cos(angle), -np.sin(angle)]))
    return (
        halves(np.stack(first)),
        second,
        second_back,
        halves(np.stack(first_back)),
        np.stack(twiddle).astype(np.float32),
    )


def split(value):
    high = value.astype(BF16)
    low = (value - high.astype(F32)).astype(BF16)
    return high, low


def dot3(left, right):
    def one(a, b):
        return jnp.dot(a, b, preferred_element_type=F32)

    return one(left[0], right[0]) + (one(left[0], right[1]) + one(left[1], right[0]))


def kernel(
    q_ref, k_ref, v_ref, h_ref, bias_ref, f1_ref, f2_ref, g2_ref, g1_ref, tw_ref, out_ref,
    q_in, k_in, v_in, h_in, f1, f2, g2, g1, tw,
    h_send, u_send, h_all, u_all, q_send, q_all, y_send, y_all, part_send, part_all,
    in_sem, h_out, u_out, h_arrived, u_arrived, twin_out, twin_arrived,
    q_out, q_arrived, part_out, part_arrived, y_out, y_arrived,
):
    s = lax.axis_index("seq")
    g = lax.axis_index("chan")
    core = lax.rem(s, 2)
    chip = lax.div(s, 2)
    twin = s + 1 - 2 * core

    pairs = [
        (h_ref, h_in),
        (k_ref, k_in),
        (v_ref, v_in),
        (q_ref, q_in),
        (f1_ref.at[core], f1),
        (tw_ref.at[core], tw),
        (f2_ref, f2),
        (g2_ref, g2),
        (g1_ref.at[core], g1),
    ]
    loads = [pltpu.make_async_copy(a, b, in_sem.at[n]) for n, (a, b) in enumerate(pairs)]
    for load in loads:
        load.start()

    barrier = pltpu.get_barrier_semaphore()

    @pl.loop(1, CHIPS)
    def _(d):
        pl.semaphore_signal(barrier, inc=1, device_id=(2 * lax.rem(chip + d, CHIPS) + core, g), device_id_type=MESH)

    pl.semaphore_signal(barrier, inc=1, device_id=(twin, g), device_id_type=MESH)

    @pl.loop(1, GROUPS)
    def _(d):
        pl.semaphore_signal(barrier, inc=1, device_id=(s, lax.rem(g + d, GROUPS)), device_id_type=MESH)

    loads[0].wait()
    row = lax.broadcasted_iota(jnp.int32, (CHIPS, 128), 0)
    lane = lax.broadcasted_iota(jnp.int32, (CHIPS, 128), 1)
    direct = jnp.zeros((CHIPS, 128), F32)
    for c in range(CHIPS):
        direct = jnp.where(row == c, bias_ref[c], direct)
    direct = jnp.where((lane == 0) & (s == 0), direct, 0.0)
    h_in[:, 0:128] = h_in[:, 0:128] + direct
    for j in range(32):
        h_send[pl.ds(j, CHIPS, stride=32), :] = h_in[:, 128 * j : 128 * j + 128]
    pl.semaphore_wait(barrier, CHIPS + GROUPS - 1)

    def outward(src, dst, out_sem, arrived):
        @pl.loop(1, CHIPS)
        def _(d):
            to = lax.rem(chip + d, CHIPS)
            pltpu.make_async_remote_copy(
                src_ref=src.at[pl.ds(pl.multiple_of(32 * to, 32), 32)],
                dst_ref=dst.at[pl.ds(pl.multiple_of(32 * s, 32), 32)],
                send_sem=out_sem,
                recv_sem=arrived.at[chip],
                device_id=(2 * to + core, g),
                device_id_type=MESH,
            ).start()

    def to_twin(array, n):
        rows = array.at[pl.ds(pl.multiple_of(32 * (2 * n + core), 32), 32)]
        return rows

    def own(src, dst, sem, arrived):
        dst[pl.ds(pl.multiple_of(32 * s, 32), 32)] = src[pl.ds(pl.multiple_of(32 * chip, 32), 32)]
        rows = to_twin(dst, chip)
        pltpu.make_async_remote_copy(
            src_ref=rows, dst_ref=rows, send_sem=sem, recv_sem=arrived, device_id=(twin, g), device_id_type=MESH
        ).start()

    def pass_on(array, arrived, n):
        @pl.loop(1, CHIPS)
        def _(d):
            source = lax.rem(chip - d + CHIPS, CHIPS)
            rows = to_twin(array, source)
            pltpu.make_async_copy(rows, rows, arrived.at[source]).wait()
            pltpu.make_async_remote_copy(
                src_ref=rows,
                dst_ref=rows,
                send_sem=twin_out.at[n],
                recv_sem=twin_arrived.at[n],
                device_id=(twin, g),
                device_id_type=MESH,
            ).start()

    def wait_bytes(array, sem):
        pltpu.make_async_copy(array, array, sem).wait()

    outward(h_send, h_all, h_out, h_arrived)
    own(h_send, h_all, twin_out.at[0], twin_arrived.at[0])

    loads[1].wait()
    loads[2].wait()
    for j in range(32):
        cols = slice(128 * j, 128 * j + 128)
        u_send[pl.ds(j, CHIPS, stride=32), :] = k_in[:, cols].astype(F32) * v_in[:, cols].astype(F32)
    outward(u_send, u_all, u_out, u_arrived)
    own(u_send, u_all, twin_out.at[1], twin_arrived.at[1])

    loads[3].wait()
    for j in range(GROUPS):
        q_send[16 * j : 16 * j + 16, :] = q_in[:, 512 * j : 512 * j + 512].astype(F32)

    for n in range(4, 9):
        loads[n].wait()

    def forward(array):
        points = jnp.concatenate([array[pl.ds(0, ROWS, stride=2), :], array[pl.ds(1, ROWS, stride=2), :]], axis=1)
        a = dot3((f1[0], f1[1]), split(points))
        re, im = a[:HALF], a[HALF:]
        b = jnp.concatenate([re * tw[0] - im * tw[1], re * tw[1] + im * tw[0]], axis=1)
        return dot3(split(b), (f2[0], f2[1]))

    pass_on(h_all, h_arrived, 0)
    wait_bytes(h_all.at[pl.ds(0, 512)], twin_arrived.at[0])
    hf = forward(h_all)

    pass_on(u_all, u_arrived, 1)

    @pl.loop(1, GROUPS)
    def _(d):
        to = lax.rem(g + d, GROUPS)
        pltpu.make_async_remote_copy(
            src_ref=q_send.at[pl.ds(pl.multiple_of(16 * to, 16), 16)],
            dst_ref=q_all.at[pl.ds(pl.multiple_of(16 * g, 16), 16)],
            send_sem=q_out,
            recv_sem=q_arrived,
            device_id=(s, to),
            device_id_type=MESH,
        ).start()

    q_all[pl.ds(pl.multiple_of(16 * g, 16), 16)] = q_send[pl.ds(pl.multiple_of(16 * g, 16), 16)]

    wait_bytes(u_all.at[pl.ds(0, 512)], twin_arrived.at[1])
    uf = forward(u_all)
    ur, ui, hr, hi = uf[:, :COLS], uf[:, COLS:], hf[:, :COLS], hf[:, COLS:]
    y = jnp.concatenate([ur * hr - ui * hi, ur * hi + ui * hr], axis=1)
    b = dot3(split(y), (g2[0], g2[1]))
    re, im = b[:, :COLS], b[:, COLS:]
    e = split(jnp.concatenate([re * tw[0] + im * tw[1], im * tw[0] - re * tw[1]], axis=0))
    part_send[...] = dot3((g1[0, HALF:], g1[1, HALF:]), e)
    exchange = pltpu.make_async_remote_copy(
        src_ref=part_send,
        dst_ref=part_all,
        send_sem=part_out,
        recv_sem=part_arrived,
        device_id=(twin, g),
        device_id_type=MESH,
    )
    exchange.start()
    mine = dot3((g1[0, :HALF], g1[1, :HALF]), e)
    wait_bytes(q_all.at[pl.ds(0, 112)], q_arrived)
    exchange.wait()
    mine = mine + part_all[...]
    for bit in range(2):
        for side in range(2):
            y_send[:, 2 * bit + side, :] = mine[128 * bit : 128 * bit + 128, 128 * side : 128 * side + 128]

    spot = chip * GROUPS + g
    channel = g * CHIPS + chip

    @pl.loop(1, CHIPS * GROUPS)
    def _(d):
        to = lax.rem(spot + d, CHIPS * GROUPS)
        pltpu.make_async_remote_copy(
            src_ref=y_send.at[to],
            dst_ref=y_all.at[channel],
            send_sem=y_out,
            recv_sem=y_arrived,
            device_id=(2 * lax.div(to, GROUPS) + core, lax.rem(to, GROUPS)),
            device_id_type=MESH,
        ).start()

    y_all[channel] = y_send[spot]
    wait_bytes(y_all.at[pl.ds(0, CHIPS * GROUPS - 1)], y_arrived)
    for j in range(4):
        cols = slice(128 * j, 128 * j + 128)
        out_ref[:, cols] = y_all[:, j, :] * q_all[:, cols]

    wait_bytes(h_send.at[pl.ds(0, 480)], h_out)
    wait_bytes(u_send.at[pl.ds(0, 480)], u_out)
    wait_bytes(h_all.at[pl.ds(0, 512)], twin_out.at[0])
    wait_bytes(u_all.at[pl.ds(0, 512)], twin_out.at[1])
    wait_bytes(q_send.at[pl.ds(0, 112)], q_out)
    wait_bytes(y_send.at[pl.ds(0, CHIPS * GROUPS - 1)], y_out)


def body(query_proj, key_proj, value_proj, filter_taps, skip_bias):
    any_space = pl.BlockSpec(memory_space=pl.ANY)
    dma = pltpu.SemaphoreType.DMA
    consts = [jnp.asarray(t) for t in tables()]
    return pl.pallas_call(
        kernel,
        out_shape=jax.ShapeDtypeStruct((128, 512), F32),
        in_specs=[any_space] * 4 + [pl.BlockSpec(memory_space=pltpu.SMEM)] + [any_space] * 5,
        out_specs=pl.BlockSpec(memory_space=pltpu.VMEM),
        scratch_shapes=[
            pltpu.VMEM((16, 4096), BF16),
            pltpu.VMEM((16, 4096), BF16),
            pltpu.VMEM((16, 4096), BF16),
            pltpu.VMEM((16, 4096), F32),
            pltpu.VMEM((2, ROWS, ROWS), BF16),
            pltpu.VMEM((2, 2 * COLS, 2 * COLS), BF16),
            pltpu.VMEM((2, 2 * COLS, 2 * COLS), BF16),
            pltpu.VMEM((2, ROWS, ROWS), BF16),
            pltpu.VMEM((2, HALF, COLS), F32),
            pltpu.VMEM((512, 128), F32),
            pltpu.VMEM((512, 128), F32),
            pltpu.VMEM((1024, 128), F32),
            pltpu.VMEM((1024, 128), F32),
            pltpu.VMEM((128, 512), F32),
            pltpu.VMEM((128, 512), F32),
            pltpu.VMEM((128, 4, 128), F32),
            pltpu.VMEM((128, 4, 128), F32),
            pltpu.VMEM((HALF, COLS), F32),
            pltpu.VMEM((HALF, COLS), F32),
            dma((9,)),
            dma,
            dma,
            dma((CHIPS,)),
            dma((CHIPS,)),
            dma((2,)),
            dma((2,)),
            dma,
            dma,
            dma,
            dma,
            dma,
            dma,
        ],
        compiler_params=pltpu.CompilerParams(
            collective_id=0, has_side_effects=True, vmem_limit_bytes=48 * 2**20
        ),
        cost_estimate=pl.CostEstimate(flops=2_400_000_000, bytes_accessed=6_000_000, transcendentals=0),
    )(query_proj, key_proj, value_proj, filter_taps, skip_bias, *consts)


def solution(mesh):
    placed = (P("chan", "seq"), P("chan", "seq"), P("chan", "seq"), P("chan", "seq"), P("chan"))
    return jax.shard_map(
        body, mesh=mesh, in_specs=placed, out_specs=P(None, ("seq", "chan")), check_vma=False
    )
```

time: 409 us -> 57.8 us (0.14)
  the two profiles are of different devices: /device:TPU:8 before, /device:TPU:32 now
where the time goes in v1:
time: 57.8 us; the launch traced here: 57.2 us
  Pallas kernels  46.9 us (81%)
  local copies, waits for them, and re-layouts  10.3 us (18%)
    pallas_call x1, Pallas kernels, body(): pl.pallas_call(kernel, out_shape=jax.ShapeDtypeStruct((128, 512), F32), i...  46.9 us
    unnamed x19, local copies, waits for them, and re-layouts  10.3 us

profile of v1, /device:TPU:32, one launch (start us, length us, event | category | flops | bytes accessed | tf_op | source)
XLA Modules:
  0.0 57.2 jit_solution(2482387822297184148)
XLA Ops:
  0.0 0.0 copy-start
  0.0 0.9 %copy-done = f32[16,4096]{1,0:T(8,128)S(1)} copy-done((f32[16,4096]{1,0:T(8,128)S(1)}, f32[16,4096]{1,0:T(8,128)}, u32[]{:S(2)}) %copy-start) | copy-done | bytes 262168
  1.0 0.0 copy-start.1
  1.0 0.9 %copy-done.1 = bf16[16,4096]{1,0:T(8,128)(2,1)S(1)} copy-done((bf16[16,4096]{1,0:T(8,128)(2,1)S(1)}, bf16[16,4096]{1,0:T(8,128)(2,1)}, u32[]{:S(2)}) %copy-start.1) | copy-done | bytes 131096
  1.9 0.0 copy-start.2
  1.9 0.9 %copy-done.2 = bf16[16,4096]{1,0:T(8,128)(2,1)S(1)} copy-done((bf16[16,4096]{1,0:T(8,128)(2,1)S(1)}, bf16[16,4096]{1,0:T(8,128)(2,1)}, u32[]{:S(2)}) %copy-start.2) | copy-done | bytes 131096
  2.8 0.0 copy-start.3
  2.8 0.9 %copy-done.3 = bf16[16,4096]{1,0:T(8,128)(2,1)S(1)} copy-done((bf16[16,4096]{1,0:T(8,128)(2,1)S(1)}, bf16[16,4096]{1,0:T(8,128)(2,1)}, u32[]{:S(2)}) %copy-start.3) | copy-done | bytes 131096
  3.7 0.0 copy-start.4
  3.7 0.7 %copy-done.4 = f32[16]{0:T(128)S(1)} copy-done((f32[16]{0:T(128)S(1)}, f32[16]{0:T(128)}, u32[]{:S(2)}) %copy-start.4) | copy-done | bytes 88
  4.3 0.0 copy-start.5
  4.3 1.6 %copy-done.5 = bf16[2,2,512,512]{3,2,1,0:T(8,128)(2,1)S(1)} copy-done((bf16[2,2,512,512]{3,2,1,0:T(8,128)(2,1)S(1)}, bf16[2,2,512,512]{3,2,1,0:T(8,128)(2,1)}, u32[]{:S(2)}) %copy-start.5) | copy-done | bytes 2097176
  5.9 0.0 copy-start.6
  5.9 1.2 %copy-done.6 = f32[2,2,256,256]{3,2,1,0:T(8,128)S(1)} copy-done((f32[2,2,256,256]{3,2,1,0:T(8,128)S(1)}, f32[2,2,256,256]{3,2,1,0:T(8,128)}, u32[]{:S(2)}) %copy-start.6) | copy-done | bytes 1048600
  7.1 0.0 copy-start.7
  7.1 1.2 %copy-done.7 = bf16[2,512,512]{2,1,0:T(8,128)(2,1)S(1)} copy-done((bf16[2,512,512]{2,1,0:T(8,128)(2,1)S(1)}, bf16[2,512,512]{2,1,0:T(8,128)(2,1)}, u32[]{:S(2)}) %copy-start.7) | copy-done | bytes 1048600
  8.4 0.0 copy-start.8
  8.4 1.2 %copy-done.8 = bf16[2,512,512]{2,1,0:T(8,128)(2,1)S(1)} copy-done((bf16[2,512,512]{2,1,0:T(8,128)(2,1)S(1)}, bf16[2,512,512]{2,1,0:T(8,128)(2,1)}, u32[]{:S(2)}) %copy-start.8) | copy-done | bytes 1048600
  9.6 46.9 %shard_map.100 = f32[128,512]{1,0:T(8,128)S(1)} custom-call(bf16[16,4096]{1,0:T(8,128)(2,1)S(1)} %copy-done.1, bf16[16,4096]{1,0:T(8,128)(2,1)S(1)} %copy-done.2, bf16[16,4096]{1,0:T(8,128)(2,1)S(1)} %copy-done.3, f32[16,4096]{1,0:T(8,128)S(1)} %copy-done, f32[16]{0:T(128)S(1)} %copy-done.4, bf16[2,2,512,512]{3,2,1,0:T(8,128)(2,1)S(1)} %copy-done.5, ...), custom_call_target="tpu_custom_call" | custom-call | flops 2400000000 | bytes 6000000 | tf_op jit(solution)/shard_map/pallas_call | solution.py:271
  56.5 0.7 %copy.12 = f32[128,512]{1,0:T(8,128)} copy(f32[128,512]{1,0:T(8,128)S(1)} %shard_map.100) | data formatting | bytes 524288
Async XLA Ops:
  0.0 0.9 %copy-start = (f32[16,4096]{1,0:T(8,128)S(1)}, f32[16,4096]{1,0:T(8,128)}, u32[]{:S(2)}) copy-start(f32[16,4096]{1,0:T(8,128)} %h_ref.1) | copy-start | bytes 786436
  1.0 0.9 %copy-start.1 = (bf16[16,4096]{1,0:T(8,128)(2,1)S(1)}, bf16[16,4096]{1,0:T(8,128)(2,1)}, u32[]{:S(2)}) copy-start(bf16[16,4096]{1,0:T(8,128)(2,1)} %q_ref.1) | copy-start | bytes 393220
  1.9 0.9 %copy-start.2 = (bf16[16,4096]{1,0:T(8,128)(2,1)S(1)}, bf16[16,4096]{1,0:T(8,128)(2,1)}, u32[]{:S(2)}) copy-start(bf16[16,4096]{1,0:T(8,128)(2,1)} %k_ref.1) | copy-start | bytes 393220
  2.8 0.9 %copy-start.3 = (bf16[16,4096]{1,0:T(8,128)(2,1)S(1)}, bf16[16,4096]{1,0:T(8,128)(2,1)}, u32[]{:S(2)}) copy-start(bf16[16,4096]{1,0:T(8,128)(2,1)} %v_ref.1) | copy-start | bytes 393220
  3.7 0.7 %copy-start.4 = (f32[16]{0:T(128)S(1)}, f32[16]{0:T(128)}, u32[]{:S(2)}) copy-start(f32[16]{0:T(128)} %bias_ref.1) | copy-start | bytes 196
  4.3 1.6 %copy-start.5 = (bf16[2,2,512,512]{3,2,1,0:T(8,128)(2,1)S(1)}, bf16[2,2,512,512]{3,2,1,0:T(8,128)(2,1)}, u32[]{:S(2)}) copy-start(bf16[2,2,512,512]{3,2,1,0:T(8,128)(2,1)} %constant.10.clone.f1_ref) | copy-start | bytes 6291460
  5.9 1.2 %copy-start.6 = (f32[2,2,256,256]{3,2,1,0:T(8,128)S(1)}, f32[2,2,256,256]{3,2,1,0:T(8,128)}, u32[]{:S(2)}) copy-start(f32[2,2,256,256]{3,2,1,0:T(8,128)} %constant.14.clone.tw_ref) | copy-start | bytes 3145732
  7.1 1.2 %copy-start.7 = (bf16[2,512,512]{2,1,0:T(8,128)(2,1)S(1)}, bf16[2,512,512]{2,1,0:T(8,128)(2,1)}, u32[]{:S(2)}) copy-start(bf16[2,512,512]{2,1,0:T(8,128)(2,1)} %constant.12.clone.g2_ref) | copy-start | bytes 3145732
  8.4 1.2 %copy-start.8 = (bf16[2,512,512]{2,1,0:T(8,128)(2,1)S(1)}, bf16[2,512,512]{2,1,0:T(8,128)(2,1)}, u32[]{:S(2)}) copy-start(bf16[2,512,512]{2,1,0:T(8,128)(2,1)} %constant.11.clone.f2_ref) | copy-start | bytes 3145732

commit v2 on v1

--- a/solution.py
+++ b/solution.py
@@ -76,7 +76,7 @@
     q_in, k_in, v_in, h_in, f1, f2, g2, g1, tw,
     h_send, u_send, h_all, u_all, q_send, q_all, y_send, y_all, part_send, part_all,
     in_sem, h_out, u_out, h_arrived, u_arrived, twin_out, twin_arrived,
-    q_out, q_arrived, part_out, part_arrived, y_out, y_arrived,
+    q_out, q_arrived, part_out, part_arrived, y_out, y_arrived, ready,
 ):
     s = lax.axis_index("seq")
     g = lax.axis_index("chan")
@@ -96,20 +96,22 @@
         (g1_ref.at[core], g1),
     ]
     loads = [pltpu.make_async_copy(a, b, in_sem.at[n]) for n, (a, b) in enumerate(pairs)]
-    for load in loads:
+    loads[0].start()
+
+    barrier = pltpu.get_barrier_semaphore()
+
+    @pl.loop(1, CHIPS)
+    def _(d):
+        pl.semaphore_signal(barrier, inc=1, device_id=(2 * lax.rem(chip + d, CHIPS) + core, g), device_id_type=MESH)
+
+    pl.semaphore_signal(barrier, inc=1, device_id=(twin, g), device_id_type=MESH)
+
+    @pl.loop(1, GROUPS)
+    def _(d):
+        pl.semaphore_signal(barrier, inc=1, device_id=(s, lax.rem(g + d, GROUPS)), device_id_type=MESH)
+
+    for load in loads[1:]:
         load.start()
-
-    barrier = pltpu.get_barrier_semaphore()
-
-    @pl.loop(1, CHIPS)
-    def _(d):
-        pl.semaphore_signal(barrier, inc=1, device_id=(2 * lax.rem(chip + d, CHIPS) + core, g), device_id_type=MESH)
-
-    pl.semaphore_signal(barrier, inc=1, device_id=(twin, g), device_id_type=MESH)
-
-    @pl.loop(1, GROUPS)
-    def _(d):
-        pl.semaphore_signal(barrier, inc=1, device_id=(s, lax.rem(g + d, GROUPS)), device_id_type=MESH)
 
     loads[0].wait()
     row = lax.broadcasted_iota(jnp.int32, (CHIPS, 128), 0)
@@ -126,7 +128,7 @@
     def outward(src, dst, out_sem, arrived):
         @pl.loop(1, CHIPS)
         def _(d):
-            to = lax.rem(chip + d, CHIPS)
+            to = chip ^ (CHIPS - d)
             pltpu.make_async_remote_copy(
                 src_ref=src.at[pl.ds(pl.multiple_of(32 * to, 32), 32)],
                 dst_ref=dst.at[pl.ds(pl.multiple_of(32 * s, 32), 32)],
@@ -150,7 +152,7 @@
     def pass_on(array, arrived, n):
         @pl.loop(1, CHIPS)
         def _(d):
-            source = lax.rem(chip - d + CHIPS, CHIPS)
+            source = chip ^ (CHIPS - d)
             rows = to_twin(array, source)
             pltpu.make_async_copy(rows, rows, arrived.at[source]).wait()
             pltpu.make_async_remote_copy(
@@ -166,6 +168,11 @@
         pltpu.make_async_copy(array, array, sem).wait()
 
     outward(h_send, h_all, h_out, h_arrived)
+
+    @pl.loop(1, GROUPS)
+    def _(d):
+        pl.semaphore_signal(ready, inc=1, device_id=(s, lax.rem(g + d, GROUPS)), device_id_type=MESH)
+
     own(h_send, h_all, twin_out.at[0], twin_arrived.at[0])
 
     loads[1].wait()
@@ -228,7 +235,6 @@
     )
     exchange.start()
     mine = dot3((g1[0, :HALF], g1[1, :HALF]), e)
-    wait_bytes(q_all.at[pl.ds(0, 112)], q_arrived)
     exchange.wait()
     mine = mine + part_all[...]
     for bit in range(2):
@@ -237,6 +243,8 @@
 
     spot = chip * GROUPS + g
     channel = g * CHIPS + chip
+
+    pl.semaphore_wait(ready, GROUPS - 1)
 
     @pl.loop(1, CHIPS * GROUPS)
     def _(d):
@@ -251,6 +259,7 @@
         ).start()
 
     y_all[channel] = y_send[spot]
+    wait_bytes(q_all.at[pl.ds(0, 112)], q_arrived)
     wait_bytes(y_all.at[pl.ds(0, CHIPS * GROUPS - 1)], y_arrived)
     for j in range(4):
         cols = slice(128 * j, 128 * j + 128)
@@ -306,9 +315,10 @@
             dma,
             dma,
             dma,
+            pltpu.SemaphoreType.REGULAR,
         ],
         compiler_params=pltpu.CompilerParams(
-            collective_id=0, has_side_effects=True, vmem_limit_bytes=48 * 2**20
+            collective_id=0, has_side_effects=True, vmem_limit_bytes=62 * 2**20
         ),
         cost_estimate=pl.CostEstimate(flops=2_400_000_000, bytes_accessed=6_000_000, transcendentals=0),
     )(query_proj, key_proj, value_proj, filter_taps, skip_bias, *consts)

time: 57.8 us -> 44.3 us (0.77)
  local copies, waits for them, and re-layouts: 10.3 us -> 1.67 us
  Pallas kernels: 46.9 us -> 42.4 us
    unnamed x19 -> x1, local copies, waits for them, and re-layouts: 10.3 us -> 1.67 us
    pallas_call x1, Pallas kernels: 46.9 us -> 42.4 us  [body(): pl.pallas_call(kernel, out_shape=jax.ShapeDtypeStruct((128, 512), F32), i...]
where the time goes in v2:
time: 44.3 us; the launch traced here: 44.1 us
  Pallas kernels  42.4 us (96%)
  local copies, waits for them, and re-layouts  1.67 us (4%)
    pallas_call x1, Pallas kernels, body(): pl.pallas_call(kernel, out_shape=jax.ShapeDtypeStruct((128, 512), F32), i...  42.4 us
    unnamed x1, local copies, waits for them, and re-layouts  1.67 us

profile of v2, /device:TPU:32, one launch (start us, length us, event | category | flops | bytes accessed | tf_op | source)
XLA Modules:
  0.0 44.1 jit_solution(8948559005756941199)
XLA Ops:
  0.0 42.4 %shard_map.100 = f32[128,512]{1,0:T(8,128)} custom-call(bf16[16,4096]{1,0:T(8,128)(2,1)} %q_ref.1, bf16[16,4096]{1,0:T(8,128)(2,1)} %k_ref.1, bf16[16,4096]{1,0:T(8,128)(2,1)} %v_ref.1, f32[16,4096]{1,0:T(8,128)} %h_ref.1, f32[16]{0:T(128)} %bias_ref.1, bf16[2,2,512,512]{3,2,1,0:T(8,128)(2,1)} %constant.10.clone.f1_ref, ...), custom_call_target="tpu_custom_call" | custom-call | flops 2400000000 | bytes 6000000 | tf_op jit(solution)/shard_map/pallas_call | solution.py:280
  42.5 1.7 %copy.12 = f32[128,512]{1,0:T(8,128)} copy(f32[128,512]{1,0:T(8,128)} %shard_map.100) | data formatting | bytes 524288

commit v3 on v2

--- a/solution.py
+++ b/solution.py
@@ -19,6 +19,9 @@
 CHIPS = 16
 GROUPS = 8
 HALF = ROWS // 2
+
+TAPS_ORDER = [4 * z + y for z in (3, 2, 0, 1) for y in (3, 2, 1, 0) if z + y]
+INPUT_ORDER = [4 * z + y for z in (1, 0, 3, 2) for y in (3, 2, 1, 0) if z + y]
 
 
 def halves(table):
@@ -72,11 +75,11 @@
 
 
 def kernel(
-    q_ref, k_ref, v_ref, h_ref, bias_ref, f1_ref, f2_ref, g2_ref, g1_ref, tw_ref, out_ref,
+    q_ref, k_ref, v_ref, h_ref, bias_ref, f1_ref, f2_ref, g2_ref, g1_ref, tw_ref, y_all, q_all,
     q_in, k_in, v_in, h_in, f1, f2, g2, g1, tw,
-    h_send, u_send, h_all, u_all, q_send, q_all, y_send, y_all, part_send, part_all,
+    h_send, u_send, h_all, u_all, q_send, y_send, part_send, part_all,
     in_sem, h_out, u_out, h_arrived, u_arrived, twin_out, twin_arrived,
-    q_out, q_arrived, part_out, part_arrived, y_out, y_arrived, ready,
+    q_out, q_arrived, part_out, part_arrived, y_out, y_arrived, ready, own_sem,
 ):
     s = lax.axis_index("seq")
     g = lax.axis_index("chan")
@@ -125,10 +128,9 @@
         h_send[pl.ds(j, CHIPS, stride=32), :] = h_in[:, 128 * j : 128 * j + 128]
     pl.semaphore_wait(barrier, CHIPS + GROUPS - 1)
 
-    def outward(src, dst, out_sem, arrived):
-        @pl.loop(1, CHIPS)
-        def _(d):
-            to = chip ^ (CHIPS - d)
+    def outward(src, dst, out_sem, arrived, order):
+        for d in order:
+            to = chip ^ d
             pltpu.make_async_remote_copy(
                 src_ref=src.at[pl.ds(pl.multiple_of(32 * to, 32), 32)],
                 dst_ref=dst.at[pl.ds(pl.multiple_of(32 * s, 32), 32)],
@@ -149,10 +151,9 @@
             src_ref=rows, dst_ref=rows, send_sem=sem, recv_sem=arrived, device_id=(twin, g), device_id_type=MESH
         ).start()
 
-    def pass_on(array, arrived, n):
-        @pl.loop(1, CHIPS)
-        def _(d):
-            source = chip ^ (CHIPS - d)
+    def pass_on(array, arrived, n, order):
+        for d in order:
+            source = chip ^ d
             rows = to_twin(array, source)
             pltpu.make_async_copy(rows, rows, arrived.at[source]).wait()
             pltpu.make_async_remote_copy(
@@ -167,7 +168,7 @@
     def wait_bytes(array, sem):
         pltpu.make_async_copy(array, array, sem).wait()
 
-    outward(h_send, h_all, h_out, h_arrived)
+    outward(h_send, h_all, h_out, h_arrived, TAPS_ORDER)
 
     @pl.loop(1, GROUPS)
     def _(d):
@@ -180,7 +181,7 @@
     for j in range(32):
         cols = slice(128 * j, 128 * j + 128)
         u_send[pl.ds(j, CHIPS, stride=32), :] = k_in[:, cols].astype(F32) * v_in[:, cols].astype(F32)
-    outward(u_send, u_all, u_out, u_arrived)
+    outward(u_send, u_all, u_out, u_arrived, INPUT_ORDER)
     own(u_send, u_all, twin_out.at[1], twin_arrived.at[1])
 
     loads[3].wait()
@@ -197,11 +198,11 @@
         b = jnp.concatenate([re * tw[0] - im * tw[1], re * tw[1] + im * tw[0]], axis=1)
         return dot3(split(b), (f2[0], f2[1]))
 
-    pass_on(h_all, h_arrived, 0)
+    pass_on(h_all, h_arrived, 0, TAPS_ORDER)
     wait_bytes(h_all.at[pl.ds(0, 512)], twin_arrived.at[0])
     hf = forward(h_all)
 
-    pass_on(u_all, u_arrived, 1)
+    pass_on(u_all, u_arrived, 1, INPUT_ORDER)
 
     @pl.loop(1, GROUPS)
     def _(d):
@@ -215,7 +216,9 @@
             device_id_type=MESH,
         ).start()
 
-    q_all[pl.ds(pl.multiple_of(16 * g, 16), 16)] = q_send[pl.ds(pl.multiple_of(16 * g, 16), 16)]
+    q_rows = pl.ds(pl.multiple_of(16 * g, 16), 16)
+    q_own = pltpu.make_async_copy(q_send.at[q_rows], q_all.at[q_rows], own_sem.at[0])
+    q_own.start()
 
     wait_bytes(u_all.at[pl.ds(0, 512)], twin_arrived.at[1])
     uf = forward(u_all)
@@ -258,30 +261,29 @@
             device_id_type=MESH,
         ).start()
 
-    y_all[channel] = y_send[spot]
-    wait_bytes(q_all.at[pl.ds(0, 112)], q_arrived)
-    wait_bytes(y_all.at[pl.ds(0, CHIPS * GROUPS - 1)], y_arrived)
-    for j in range(4):
-        cols = slice(128 * j, 128 * j + 128)
-        out_ref[:, cols] = y_all[:, j, :] * q_all[:, cols]
-
+    y_own = pltpu.make_async_copy(y_send.at[spot], y_all.at[channel], own_sem.at[1])
+    y_own.start()
     wait_bytes(h_send.at[pl.ds(0, 480)], h_out)
     wait_bytes(u_send.at[pl.ds(0, 480)], u_out)
     wait_bytes(h_all.at[pl.ds(0, 512)], twin_out.at[0])
     wait_bytes(u_all.at[pl.ds(0, 512)], twin_out.at[1])
     wait_bytes(q_send.at[pl.ds(0, 112)], q_out)
     wait_bytes(y_send.at[pl.ds(0, CHIPS * GROUPS - 1)], y_out)
+    q_own.wait()
+    y_own.wait()
+    wait_bytes(q_all.at[pl.ds(0, 112)], q_arrived)
+    wait_bytes(y_all.at[pl.ds(0, CHIPS * GROUPS - 1)], y_arrived)
 
 
 def body(query_proj, key_proj, value_proj, filter_taps, skip_bias):
     any_space = pl.BlockSpec(memory_space=pl.ANY)
     dma = pltpu.SemaphoreType.DMA
     consts = [jnp.asarray(t) for t in tables()]
-    return pl.pallas_call(
+    y, q = pl.pallas_call(
         kernel,
-        out_shape=jax.ShapeDtypeStruct((128, 512), F32),
+        out_shape=[jax.ShapeDtypeStruct((128, 4, 128), F32), jax.ShapeDtypeStruct((128, 512), F32)],
         in_specs=[any_space] * 4 + [pl.BlockSpec(memory_space=pltpu.SMEM)] + [any_space] * 5,
-        out_specs=pl.BlockSpec(memory_space=pltpu.VMEM),
+        out_specs=[any_space] * 2,
         scratch_shapes=[
             pltpu.VMEM((16, 4096), BF16),
             pltpu.VMEM((16, 4096), BF16),
@@ -297,8 +299,6 @@
             pltpu.VMEM((1024, 128), F32),
             pltpu.VMEM((1024, 128), F32),
             pltpu.VMEM((128, 512), F32),
-            pltpu.VMEM((128, 512), F32),
-            pltpu.VMEM((128, 4, 128), F32),
             pltpu.VMEM((128, 4, 128), F32),
             pltpu.VMEM((HALF, COLS), F32),
             pltpu.VMEM((HALF, COLS), F32),
@@ -316,12 +316,14 @@
             dma,
             dma,
             pltpu.SemaphoreType.REGULAR,
+            dma((2,)),
         ],
         compiler_params=pltpu.CompilerParams(
             collective_id=0, has_side_effects=True, vmem_limit_bytes=62 * 2**20
         ),
         cost_estimate=pl.CostEstimate(flops=2_400_000_000, bytes_accessed=6_000_000, transcendentals=0),
     )(query_proj, key_proj, value_proj, filter_taps, skip_bias, *consts)
+    return y.reshape(128, 512) * q
 
 
 def solution(mesh):

time: 44.3 us -> 42 us (0.948)
  Pallas kernels: 42.4 us -> 39.9 us
  other arithmetic: 0 us -> 1.77 us
  local copies, waits for them, and re-layouts: 1.67 us -> 0 us
    pallas_call x1, Pallas kernels: 42.4 us -> 39.9 us  [body(): pl.pallas_call(kernel, out_shape=[jax.ShapeDtypeStruct((128, 4, 128), F32...]
    mul x0 -> x1, other arithmetic: none -> 1.77 us  [body(): return y.reshape(128, 512) * q]
    unnamed x1 -> x0, local copies, waits for them, and re-layouts: 1.67 us -> none
where the time goes in v3:
time: 42 us; the launch traced here: 41.6 us
  Pallas kernels  39.9 us (95%)
  other arithmetic  1.77 us (4%)
    pallas_call x1, Pallas kernels, body(): pl.pallas_call(kernel, out_shape=[jax.ShapeDtypeStruct((128, 4, 128), F32...  39.9 us
    mul x1, other arithmetic, body(): return y.reshape(128, 512) * q  1.77 us

profile of v3, /device:TPU:32, one launch (start us, length us, event | category | flops | bytes accessed | tf_op | source)
XLA Modules:
  0.0 41.6 jit_solution(17011093296600105607)
XLA Ops:
  0.0 39.9 %shard_map.100 = (f32[128,4,128]{2,1,0:T(4,128)}, f32[128,512]{1,0:T(8,128)}) custom-call(bf16[16,4096]{1,0:T(8,128)(2,1)} %q_ref.1, bf16[16,4096]{1,0:T(8,128)(2,1)} %k_ref.1, bf16[16,4096]{1,0:T(8,128)(2,1)} %v_ref.1, f32[16,4096]{1,0:T(8,128)} %h_ref.1, f32[16]{0:T(128)} %bias_ref.1, bf16[2,2,512,512]{3,2,1,0:T(8,128)(2,1)} %constant.10.clone.f1_ref, ...), custom_call_target="tpu_custom_call" | custom-call | flops 2400000000 | bytes 6000000 | tf_op jit(solution)/shard_map/pallas_call | solution.py:282
  39.9 1.8 %bitcast_multiply_fusion = f32[128,512]{1,0:T(8,128)} fusion(f32[128,512]{1,0:T(8,128)} %get-tuple-element.8, f32[16,8,4,128]{3,2,1,0:T(4,128)} %bitcast.3), kind=kLoop, calls=%fused_computation | loop fusion | flops 65536 | bytes 786432 | tf_op jit(solution)/shard_map/mul | solution.py:326

commit v4 on v3

--- a/solution.py
+++ b/solution.py
@@ -75,10 +75,10 @@
 
 
 def kernel(
-    q_ref, k_ref, v_ref, h_ref, bias_ref, f1_ref, f2_ref, g2_ref, g1_ref, tw_ref, y_all, q_all,
+    q_ref, k_ref, v_ref, h_ref, b_ref, f1_ref, f2_ref, g2_ref, g1_ref, tw_ref, y_all, q_all,
     q_in, k_in, v_in, h_in, f1, f2, g2, g1, tw,
     h_send, u_send, h_all, u_all, q_send, y_send, part_send, part_all,
-    in_sem, h_out, u_out, h_arrived, u_arrived, twin_out, twin_arrived,
+    bias_ref, in_sem, h_out, u_out, h_arrived, u_arrived, twin_out, twin_arrived,
     q_out, q_arrived, part_out, part_arrived, y_out, y_arrived, ready, own_sem,
 ):
     s = lax.axis_index("seq")
@@ -97,9 +97,11 @@
         (f2_ref, f2),
         (g2_ref, g2),
         (g1_ref.at[core], g1),
+        (b_ref, bias_ref),
     ]
     loads = [pltpu.make_async_copy(a, b, in_sem.at[n]) for n, (a, b) in enumerate(pairs)]
     loads[0].start()
+    loads[9].start()
 
     barrier = pltpu.get_barrier_semaphore()
 
@@ -113,10 +115,11 @@
     def _(d):
         pl.semaphore_signal(barrier, inc=1, device_id=(s, lax.rem(g + d, GROUPS)), device_id_type=MESH)
 
-    for load in loads[1:]:
+    for load in loads[1:9]:
         load.start()
 
     loads[0].wait()
+    loads[9].wait()
     row = lax.broadcasted_iota(jnp.int32, (CHIPS, 128), 0)
     lane = lax.broadcasted_iota(jnp.int32, (CHIPS, 128), 1)
     direct = jnp.zeros((CHIPS, 128), F32)
@@ -188,6 +191,24 @@
     for j in range(GROUPS):
         q_send[16 * j : 16 * j + 16, :] = q_in[:, 512 * j : 512 * j + 512].astype(F32)
 
+    def send_query(z_half, first):
+        @pl.loop(first, GROUPS // 2)
+        def _(d):
+            to = 2 * lax.rem(lax.div(g, 2) + d, GROUPS // 2) + z_half
+            pltpu.make_async_remote_copy(
+                src_ref=q_send.at[pl.ds(pl.multiple_of(16 * to, 16), 16)],
+                dst_ref=q_all.at[pl.ds(pl.multiple_of(16 * g, 16), 16)],
+                send_sem=q_out,
+                recv_sem=q_arrived,
+                device_id=(s, to),
+                device_id_type=MESH,
+            ).start()
+
+    q_rows = pl.ds(pl.multiple_of(16 * g, 16), 16)
+    q_own = pltpu.make_async_copy(q_send.at[q_rows], q_all.at[q_rows], own_sem.at[0])
+    q_own.start()
+    send_query(lax.rem(g, 2), 1)
+
     for n in range(4, 9):
         loads[n].wait()
 
@@ -203,22 +224,7 @@
     hf = forward(h_all)
 
     pass_on(u_all, u_arrived, 1, INPUT_ORDER)
-
-    @pl.loop(1, GROUPS)
-    def _(d):
-        to = lax.rem(g + d, GROUPS)
-        pltpu.make_async_remote_copy(
-            src_ref=q_send.at[pl.ds(pl.multiple_of(16 * to, 16), 16)],
-            dst_ref=q_all.at[pl.ds(pl.multiple_of(16 * g, 16), 16)],
-            send_sem=q_out,
-            recv_sem=q_arrived,
-            device_id=(s, to),
-            device_id_type=MESH,
-        ).start()
-
-    q_rows = pl.ds(pl.multiple_of(16 * g, 16), 16)
-    q_own = pltpu.make_async_copy(q_send.at[q_rows], q_all.at[q_rows], own_sem.at[0])
-    q_own.start()
+    send_query(1 - lax.rem(g, 2), 0)
 
     wait_bytes(u_all.at[pl.ds(0, 512)], twin_arrived.at[1])
     uf = forward(u_all)
@@ -282,7 +288,7 @@
     y, q = pl.pallas_call(
         kernel,
         out_shape=[jax.ShapeDtypeStruct((128, 4, 128), F32), jax.ShapeDtypeStruct((128, 512), F32)],
-        in_specs=[any_space] * 4 + [pl.BlockSpec(memory_space=pltpu.SMEM)] + [any_space] * 5,
+        in_specs=[any_space] * 10,
         out_specs=[any_space] * 2,
         scratch_shapes=[
             pltpu.VMEM((16, 4096), BF16),
@@ -302,7 +308,8 @@
             pltpu.VMEM((128, 4, 128), F32),
             pltpu.VMEM((HALF, COLS), F32),
             pltpu.VMEM((HALF, COLS), F32),
-            dma((9,)),
+            pltpu.SMEM((CHIPS,), F32),
+            dma((10,)),
             dma,
             dma,
             dma((CHIPS,)),

time: 42 us -> 41.3 us (0.983)
  Pallas kernels: 39.9 us -> 39.4 us
    pallas_call x1, Pallas kernels: 39.9 us -> 39.4 us  [body(): pl.pallas_call(kernel, out_shape=[jax.ShapeDtypeStruct((128, 4, 128), F32...]
where the time goes in v4:
time: 41.3 us; the launch traced here: 41.2 us
  Pallas kernels  39.4 us (95%)
  other arithmetic  1.77 us (4%)
    pallas_call x1, Pallas kernels, body(): pl.pallas_call(kernel, out_shape=[jax.ShapeDtypeStruct((128, 4, 128), F32...  39.4 us
    mul x1, other arithmetic, body(): return y.reshape(128, 512) * q  1.77 us

profile of v4, /device:TPU:32, one launch (start us, length us, event | category | flops | bytes accessed | tf_op | source)
XLA Modules:
  0.0 41.2 jit_solution(15098697842368140632)
XLA Ops:
  0.0 39.4 %shard_map.100 = (f32[128,4,128]{2,1,0:T(4,128)}, f32[128,512]{1,0:T(8,128)}) custom-call(bf16[16,4096]{1,0:T(8,128)(2,1)} %q_ref.1, bf16[16,4096]{1,0:T(8,128)(2,1)} %k_ref.1, bf16[16,4096]{1,0:T(8,128)(2,1)} %v_ref.1, f32[16,4096]{1,0:T(8,128)} %h_ref.1, f32[16]{0:T(128)} %b_ref.1, bf16[2,2,512,512]{3,2,1,0:T(8,128)(2,1)} %constant.10.clone.f1_ref, ...), custom_call_target="tpu_custom_call" | custom-call | flops 2400000000 | bytes 6000000 | tf_op jit(solution)/shard_map/pallas_call | solution.py:288
  39.4 1.8 %bitcast_multiply_fusion = f32[128,512]{1,0:T(8,128)} fusion(f32[128,512]{1,0:T(8,128)} %get-tuple-element.8, f32[16,8,4,128]{3,2,1,0:T(4,128)} %bitcast.3), kind=kLoop, calls=%fused_computation | loop fusion | flops 65536 | bytes 786432 | tf_op jit(solution)/shard_map/mul | solution.py:333

commit v5 on v4

--- a/solution.py
+++ b/solution.py
@@ -287,7 +287,7 @@
     consts = [jnp.asarray(t) for t in tables()]
     y, q = pl.pallas_call(
         kernel,
-        out_shape=[jax.ShapeDtypeStruct((128, 4, 128), F32), jax.ShapeDtypeStruct((128, 512), F32)],
+        out_shape=[pltpu.VMEM((128, 4, 128), F32), pltpu.VMEM((128, 512), F32)],
         in_specs=[any_space] * 10,
         out_specs=[any_space] * 2,
         scratch_shapes=[
@@ -326,7 +326,7 @@
             dma((2,)),
         ],
         compiler_params=pltpu.CompilerParams(
-            collective_id=0, has_side_effects=True, vmem_limit_bytes=62 * 2**20
+            collective_id=0, has_side_effects=True, vmem_limit_bytes=107 * 2**19
         ),
         cost_estimate=pl.CostEstimate(flops=2_400_000_000, bytes_accessed=6_000_000, transcendentals=0),
     )(query_proj, key_proj, value_proj, filter_taps, skip_bias, *consts)

time: 41.3 us -> 40 us (0.969)
  other arithmetic: 1.77 us -> 0.74 us
    mul x1, other arithmetic: 1.77 us -> 0.74 us  [body(): return y.reshape(128, 512) * q]
where the time goes in v5:
time: 40 us; the launch traced here: 39.9 us
  Pallas kernels  39.2 us (98%)
  other arithmetic  0.74 us (2%)
    pallas_call x1, Pallas kernels, body(): pl.pallas_call(kernel, out_shape=[pltpu.VMEM((128, 4, 128), F32), pltpu.V...  39.2 us

profile of v5, /device:TPU:32, one launch (start us, length us, event | category | flops | bytes accessed | tf_op | source)
XLA Modules:
  0.0 39.9 jit_solution(9467820290980833338)
XLA Ops:
  0.0 39.2 %shard_map.100 = (f32[128,4,128]{2,1,0:T(4,128)S(1)}, f32[128,512]{1,0:T(8,128)S(1)}) custom-call(bf16[16,4096]{1,0:T(8,128)(2,1)} %q_ref.1, bf16[16,4096]{1,0:T(8,128)(2,1)} %k_ref.1, bf16[16,4096]{1,0:T(8,128)(2,1)} %v_ref.1, f32[16,4096]{1,0:T(8,128)} %h_ref.1, f32[16]{0:T(128)} %b_ref.1, bf16[2,2,512,512]{3,2,1,0:T(8,128)(2,1)} %constant.10.clone.f1_ref, ...), custom_call_target="tpu_custom_call" | custom-call | flops 2400000000 | bytes 6000000 | tf_op jit(solution)/shard_map/pallas_call | solution.py:288
  39.2 0.7 %bitcast_multiply_fusion = f32[128,512]{1,0:T(8,128)} fusion(f32[128,512]{1,0:T(8,128)S(1)} %get-tuple-element.8, f32[16,8,4,128]{3,2,1,0:T(4,128)S(1)} %bitcast.3), kind=kLoop, calls=%fused_computation | loop fusion | flops 65536 | bytes 786432 | tf_op jit(solution)/shard_map/mul | solution.py:333

commit v6 on v5

--- a/solution.py
+++ b/solution.py
@@ -128,7 +128,7 @@
     direct = jnp.where((lane == 0) & (s == 0), direct, 0.0)
     h_in[:, 0:128] = h_in[:, 0:128] + direct
     for j in range(32):
-        h_send[pl.ds(j, CHIPS, stride=32), :] = h_in[:, 128 * j : 128 * j + 128]
+        h_send[pl.ds(16 * (j % 2) + j // 2, CHIPS, stride=32), :] = h_in[:, 128 * j : 128 * j + 128]
     pl.semaphore_wait(barrier, CHIPS + GROUPS - 1)
 
     def outward(src, dst, out_sem, arrived, order):
@@ -183,7 +183,7 @@
     loads[2].wait()
     for j in range(32):
         cols = slice(128 * j, 128 * j + 128)
-        u_send[pl.ds(j, CHIPS, stride=32), :] = k_in[:, cols].astype(F32) * v_in[:, cols].astype(F32)
+        u_send[pl.ds(16 * (j % 2) + j // 2, CHIPS, stride=32), :] = k_in[:, cols].astype(F32) * v_in[:, cols].astype(F32)
     outward(u_send, u_all, u_out, u_arrived, INPUT_ORDER)
     own(u_send, u_all, twin_out.at[1], twin_arrived.at[1])
 
@@ -213,7 +213,11 @@
         loads[n].wait()
 
     def forward(array):
-        points = jnp.concatenate([array[pl.ds(0, ROWS, stride=2), :], array[pl.ds(1, ROWS, stride=2), :]], axis=1)
+        halves_of = [
+            jnp.concatenate([array[32 * n + 16 * odd : 32 * n + 16 * odd + 16, :] for n in range(2 * CHIPS)], axis=0)
+            for odd in range(2)
+        ]
+        points = jnp.concatenate(halves_of, axis=1)
         a = dot3((f1[0], f1[1]), split(points))
         re, im = a[:HALF], a[HALF:]
         b = jnp.concatenate([re * tw[0] - im * tw[1], re * tw[1] + im * tw[0]], axis=1)
@@ -223,8 +227,9 @@
     wait_bytes(h_all.at[pl.ds(0, 512)], twin_arrived.at[0])
     hf = forward(h_all)
 
-    pass_on(u_all, u_arrived, 1, INPUT_ORDER)
+    pass_on(u_all, u_arrived, 1, INPUT_ORDER[:-2])
     send_query(1 - lax.rem(g, 2), 0)
+    pass_on(u_all, u_arrived, 1, INPUT_ORDER[-2:])
 
     wait_bytes(u_all.at[pl.ds(0, 512)], twin_arrived.at[1])
     uf = forward(u_all)
@@ -255,7 +260,7 @@
 
     pl.semaphore_wait(ready, GROUPS - 1)
 
-    @pl.loop(1, CHIPS * GROUPS)
+    @pl.loop(1, CHIPS * GROUPS, unroll=4)
     def _(d):
         to = lax.rem(spot + d, CHIPS * GROUPS)
         pltpu.make_async_remote_copy(

time: 40 us -> 40.1 us (level)
  no operation moved by 1% of the time
where the time goes in v6:
time: 40.1 us; the launch traced here: 40 us
  Pallas kernels  39.3 us (98%)
  other arithmetic  0.74 us (2%)
    pallas_call x1, Pallas kernels, body(): pl.pallas_call(kernel, out_shape=[pltpu.VMEM((128, 4, 128), F32), pltpu.V...  39.3 us

profile of v6, /device:TPU:32, one launch (start us, length us, event | category | flops | bytes accessed | tf_op | source)
XLA Modules:
  0.0 40.0 jit_solution(13118412500454116602)
XLA Ops:
  0.0 39.3 %shard_map.100 = (f32[128,4,128]{2,1,0:T(4,128)S(1)}, f32[128,512]{1,0:T(8,128)S(1)}) custom-call(bf16[16,4096]{1,0:T(8,128)(2,1)} %q_ref.1, bf16[16,4096]{1,0:T(8,128)(2,1)} %k_ref.1, bf16[16,4096]{1,0:T(8,128)(2,1)} %v_ref.1, f32[16,4096]{1,0:T(8,128)} %h_ref.1, f32[16]{0:T(128)} %b_ref.1, bf16[2,2,512,512]{3,2,1,0:T(8,128)(2,1)} %constant.10.clone.f1_ref, ...), custom_call_target="tpu_custom_call" | custom-call | flops 2400000000 | bytes 6000000 | tf_op jit(solution)/shard_map/pallas_call | solution.py:293
  39.3 0.7 %bitcast_multiply_fusion = f32[128,512]{1,0:T(8,128)} fusion(f32[128,512]{1,0:T(8,128)S(1)} %get-tuple-element.8, f32[16,8,4,128]{3,2,1,0:T(4,128)S(1)} %bitcast.3), kind=kLoop, calls=%fused_computation | loop fusion | flops 65536 | bytes 786432 | tf_op jit(solution)/shard_map/mul | solution.py:338

commit v7 on v6

--- a/solution.py
+++ b/solution.py
@@ -262,7 +262,8 @@
 
     @pl.loop(1, CHIPS * GROUPS, unroll=4)
     def _(d):
-        to = lax.rem(spot + d, CHIPS * GROUPS)
+        step = jnp.where(d <= 64, 2 * d - 1, 2 * (d - 64))
+        to = lax.rem(spot + step, CHIPS * GROUPS)
         pltpu.make_async_remote_copy(
             src_ref=y_send.at[to],
             dst_ref=y_all.at[channel],

time: 40.1 us -> 39.6 us (0.988)
  Pallas kernels: 39.3 us -> 38.7 us
    pallas_call x1, Pallas kernels: 39.3 us -> 38.7 us  [body(): pl.pallas_call(kernel, out_shape=[pltpu.VMEM((128, 4, 128), F32), pltpu.V...]
where the time goes in v7:
time: 39.6 us; the launch traced here: 39.5 us
  Pallas kernels  38.7 us (98%)
  other arithmetic  0.74 us (2%)
    pallas_call x1, Pallas kernels, body(): pl.pallas_call(kernel, out_shape=[pltpu.VMEM((128, 4, 128), F32), pltpu.V...  38.7 us

profile of v7, /device:TPU:32, one launch (start us, length us, event | category | flops | bytes accessed | tf_op | source)
XLA Modules:
  0.0 39.5 jit_solution(5644674986789661693)
XLA Ops:
  0.0 38.7 %shard_map.100 = (f32[128,4,128]{2,1,0:T(4,128)S(1)}, f32[128,512]{1,0:T(8,128)S(1)}) custom-call(bf16[16,4096]{1,0:T(8,128)(2,1)} %q_ref.1, bf16[16,4096]{1,0:T(8,128)(2,1)} %k_ref.1, bf16[16,4096]{1,0:T(8,128)(2,1)} %v_ref.1, f32[16,4096]{1,0:T(8,128)} %h_ref.1, f32[16]{0:T(128)} %b_ref.1, bf16[2,2,512,512]{3,2,1,0:T(8,128)(2,1)} %constant.10.clone.f1_ref, ...), custom_call_target="tpu_custom_call" | custom-call | flops 2400000000 | bytes 6000000 | tf_op jit(solution)/shard_map/pallas_call | solution.py:294
  38.8 0.7 %bitcast_multiply_fusion = f32[128,512]{1,0:T(8,128)} fusion(f32[128,512]{1,0:T(8,128)S(1)} %get-tuple-element.8, f32[16,8,4,128]{3,2,1,0:T(4,128)S(1)} %bitcast.3), kind=kLoop, calls=%fused_computation | loop fusion | flops 65536 | bytes 786432 | tf_op jit(solution)/shard_map/mul | solution.py:339

commit v8 on v7

--- a/solution.py
+++ b/solution.py
@@ -227,9 +227,9 @@
     wait_bytes(h_all.at[pl.ds(0, 512)], twin_arrived.at[0])
     hf = forward(h_all)
 
-    pass_on(u_all, u_arrived, 1, INPUT_ORDER[:-2])
+    pass_on(u_all, u_arrived, 1, INPUT_ORDER[:-4])
     send_query(1 - lax.rem(g, 2), 0)
-    pass_on(u_all, u_arrived, 1, INPUT_ORDER[-2:])
+    pass_on(u_all, u_arrived, 1, INPUT_ORDER[-4:])
 
     wait_bytes(u_all.at[pl.ds(0, 512)], twin_arrived.at[1])
     uf = forward(u_all)

time: 39.6 us -> 39.4 us (level)
  no operation moved by 1% of the time
where the time goes in v8:
time: 39.4 us; the launch traced here: 39.2 us
  Pallas kernels  38.5 us (98%)
  other arithmetic  0.74 us (2%)
    pallas_call x1, Pallas kernels, body(): pl.pallas_call(kernel, out_shape=[pltpu.VMEM((128, 4, 128), F32), pltpu.V...  38.5 us

profile of v8, /device:TPU:32, one launch (start us, length us, event | category | flops | bytes accessed | tf_op | source)
XLA Modules:
  0.0 39.2 jit_solution(5663582041897030071)
XLA Ops:
  0.0 38.5 %shard_map.100 = (f32[128,4,128]{2,1,0:T(4,128)S(1)}, f32[128,512]{1,0:T(8,128)S(1)}) custom-call(bf16[16,4096]{1,0:T(8,128)(2,1)} %q_ref.1, bf16[16,4096]{1,0:T(8,128)(2,1)} %k_ref.1, bf16[16,4096]{1,0:T(8,128)(2,1)} %v_ref.1, f32[16,4096]{1,0:T(8,128)} %h_ref.1, f32[16]{0:T(128)} %b_ref.1, bf16[2,2,512,512]{3,2,1,0:T(8,128)(2,1)} %constant.10.clone.f1_ref, ...), custom_call_target="tpu_custom_call" | custom-call | flops 2400000000 | bytes 6000000 | tf_op jit(solution)/shard_map/pallas_call | solution.py:294
  38.5 0.7 %bitcast_multiply_fusion = f32[128,512]{1,0:T(8,128)} fusion(f32[128,512]{1,0:T(8,128)S(1)} %get-tuple-element.8, f32[16,8,4,128]{3,2,1,0:T(4,128)S(1)} %bitcast.3), kind=kLoop, calls=%fused_computation | loop fusion | flops 65536 | bytes 786432 | tf_op jit(solution)/shard_map/mul | solution.py:339
